TPU v7x, 128 devices: a whole 4x4x4 slice. The times are simulated.
128 devices in a mesh: ctx: 16 (over x, z), fsdp: 8 (over y, core).
Axes of the slice: x: 4, y: 4, z: 4, core: 2. Of those that a mesh axis runs over, the one named last changes fastest.
Arguments:
- tokens: bfloat16 [8, 4096, 768], P('fsdp', 'ctx'), may hold values from -6 to 6
- segments: int32 [8, 4096], P('fsdp', 'ctx'), may hold values from 0 to 2, as said below
- routes: int32 [8, 4096, 2], P('fsdp', 'ctx'), may hold values from 0 to 15, all different within a row; in each aligned block of 256 rows (0 to 255, 256 to 511, ..., all dimensions but the last counted through in order) at most 48 rows name the same one
- w_qkv: bfloat16 [768, 2304], P(('ctx', 'fsdp')), may hold values from -0.21875 to 0.21875
- w_out: bfloat16 [768, 768], P(('ctx', 'fsdp')), may hold values from -1.75 to 1.75
- w_router: bfloat16 [768, 16], P(('ctx', 'fsdp')), may hold values from -0.21875 to 0.21875
- shared_in: bfloat16 [768, 4096], P(('ctx', 'fsdp')), may hold values from -0.21875 to 0.21875
- shared_down: bfloat16 [2048, 768], P(('ctx', 'fsdp')), may hold values from -0.125 to 0.125
- attn_gain: bfloat16 [768], P(('ctx', 'fsdp')), may hold values from 0.5 to 1.5
- ffn_gain: bfloat16 [768], P(('ctx', 'fsdp')), may hold values from 0.5 to 1.5
- expert_in: bfloat16 [16, 768, 4096], P('ctx', 'fsdp'), may hold values from -0.21875 to 0.21875
- expert_down: bfloat16 [16, 2048, 768], P('ctx', 'fsdp'), may hold values from -0.125 to 0.125
- cotangent: bfloat16 [8, 4096, 768], P('fsdp', 'ctx'), may hold values from -6 to 6
Outputs:
- mixed: bfloat16 [8, 4096, 768], P('fsdp', 'ctx')
- input_grad: float32 [8, 4096, 768], P('fsdp', 'ctx')
- grad_w_qkv: float32 [768, 2304], P(('ctx', 'fsdp'))
- grad_w_out: float32 [768, 768], P(('ctx', 'fsdp'))
- grad_w_router: float32 [768, 16], P(('ctx', 'fsdp'))
- grad_shared_in: float32 [768, 4096], P(('ctx', 'fsdp'))
- grad_shared_down: float32 [2048, 768], P(('ctx', 'fsdp'))
- grad_attn_gain: float32 [768], P(('ctx', 'fsdp'))
- grad_ffn_gain: float32 [768], P(('ctx', 'fsdp'))
- grad_expert_in: float32 [16, 768, 4096], P('ctx', 'fsdp')
- grad_expert_down: float32 [16, 2048, 768], P('ctx', 'fsdp')
Inputs may be any that keep to these rules, and one draw needn't show every extreme that they name: `segments`: segment numbers never fall along a sequence; document 1 begins within the first 256 positions and ends within the last 256; documents 0 and 2 are not empty. `routes`: A token's 2 experts differ; among the rows of one device no expert is named more than 48 times, and in some device's rows some expert exactly 48 times.
All inputs are finite; a program needn't handle non-finite values.
Results may differ from a plain program's by a relative error of at most 0.023.
Values may be sent and summed in bfloat16 or wider, within the bound.
No kernel may reach another device: no remote copies, remote signals or barrier semaphores. Data moves between devices by JAX's collectives and lax.ppermute only.
A program may use at most 256 MiB of HBM per device.

v0:
```python
import jax
import jax.numpy as jnp
from jax import lax
from jax.sharding import PartitionSpec as P

HEADS = 12
HEAD_DIM = 64
TOPK = 2
WIN = 1024


EPSILON = 1e-06


def shifted(value, axis, steps):
    count = lax.axis_size(axis)
    leading, last = (max(0, -steps), min(count, count - steps))
    return lax.ppermute(value, axis, [(source, source + steps) for source in range(leading, last)])


def rms_scale(values):
    return lax.rsqrt(jnp.mean(values * values, axis=-1, keepdims=True) + EPSILON)


def rotary_table(local_rows, offset, head_width):
    half_width = head_width // 2
    frequency = jnp.exp(
        -jnp.log(10000.0) * (2.0 * jnp.arange(half_width, dtype=jnp.float32) / head_width)
    )
    places = (offset + jnp.arange(local_rows, dtype=jnp.int32)).astype(jnp.float32)
    angles = places[:, None] * frequency[None, :]
    return (jnp.cos(angles)[:, None, :], jnp.sin(angles)[:, None, :])


def rotate(values, cosine_table, sine_table):
    half_width = values.shape[-1] // 2
    front_half = values[..., :half_width]
    back_half = values[..., half_width:]
    return jnp.concatenate(
        [
            front_half * cosine_table - back_half * sine_table,
            back_half * cosine_table + front_half * sine_table,
        ],
        axis=-1,
    )


def rotate_back(gradient, cosine_table, sine_table):
    half_width = gradient.shape[-1] // 2
    front_half = gradient[..., :half_width]
    back_half = gradient[..., half_width:]
    return jnp.concatenate(
        [
            front_half * cosine_table + back_half * sine_table,
            back_half * cosine_table - front_half * sine_table,
        ],
        axis=-1,
    )


def silu_slope(values):
    sigmoid_part = jax.nn.sigmoid(values)
    return sigmoid_part * (1.0 + values * (1.0 - sigmoid_part))


def norm_back(dnormed, values, row_scale, gain_row):
    weighted = dnormed * gain_row
    dvalues = row_scale * weighted - values * row_scale**3 * jnp.mean(
        weighted * values, axis=-1, keepdims=True
    )
    dgain = jnp.sum(dnormed * values * row_scale, axis=0)
    return (dvalues, dgain)


def window_scores(queries, key_heads, allowed, score_scale):
    scores = (
        jnp.einsum("qhd,khd->hqk", queries, key_heads, preferred_element_type=jnp.float32)
        * score_scale
    )
    return jnp.where(allowed[None], scores, -1e30)


def per_device(
    tokens,
    segments,
    routes,
    w_qkv,
    w_out,
    w_router,
    shared_in,
    shared_down,
    attn_gain,
    ffn_gain,
    expert_in,
    expert_down,
    cotangent,
):
    ctx_count = lax.axis_size("ctx")
    ctx_index = lax.axis_index("ctx")
    local_rows = tokens.shape[1]
    model_width = tokens.shape[2]
    reach_back = max(1, WIN // local_rows)
    capacity = max(2, 3 * local_rows * TOPK // (2 * ctx_count))
    score_scale = HEAD_DIM ** (-0.5)
    bfloat = jnp.bfloat16
    single = jnp.float32
    dense_full = (
        lax.all_gather(w_qkv, ("ctx", "fsdp"), axis=0, tiled=True),
        lax.all_gather(w_out, ("ctx", "fsdp"), axis=0, tiled=True),
        lax.all_gather(w_router, ("ctx", "fsdp"), axis=0, tiled=True),
        lax.all_gather(shared_in, ("ctx", "fsdp"), axis=0, tiled=True),
        lax.all_gather(shared_down, ("ctx", "fsdp"), axis=0, tiled=True),
        lax.all_gather(attn_gain, ("ctx", "fsdp"), axis=0, tiled=True),
        lax.all_gather(ffn_gain, ("ctx", "fsdp"), axis=0, tiled=True),
    )
    expert_full = (
        lax.all_gather(expert_in, "fsdp", axis=1, tiled=True),
        lax.all_gather(expert_down, "fsdp", axis=1, tiled=True),
    )
    full_qkv, full_out, full_router, full_shared_in, full_shared_down, gain_attn, gain_ffn = (
        dense_full
    )
    expert_up = expert_full[0][0]
    expert_back = expert_full[1][0]
    input_rows = tokens[0].astype(single)
    segment_own = segments[0]
    route_own = routes[0]
    gain_one = gain_attn.astype(single)
    gain_two = gain_ffn.astype(single)
    scale_one = rms_scale(input_rows)
    first_normalized = (input_rows * scale_one * gain_one).astype(bfloat)
    projected_output = jnp.dot(first_normalized, full_qkv, preferred_element_type=single)
    cosine_table, sine_table = rotary_table(local_rows, ctx_index * local_rows, HEAD_DIM)
    queries = rotate(
        projected_output[:, :model_width].reshape(local_rows, HEADS, HEAD_DIM),
        cosine_table,
        sine_table,
    ).astype(bfloat)
    key_own = (
        rotate(
            projected_output[:, model_width : 2 * model_width].reshape(local_rows, HEADS, HEAD_DIM),
            cosine_table,
            sine_table,
        )
        .astype(bfloat)
        .reshape(local_rows, model_width)
    )
    value_own = projected_output[:, 2 * model_width :].astype(bfloat)
    key_value = jnp.concatenate([key_own, value_own], axis=1)
    earlier_pairs = []
    earlier_segments = []
    for distance in range(reach_back, 0, -1):
        moved_pair, moved_segment = shifted((key_value, segment_own), "ctx", distance)
        earlier_pairs.append(moved_pair)
        earlier_segments.append(moved_segment)
    all_pairs = jnp.concatenate(earlier_pairs + [key_value], axis=0)
    all_segments = jnp.concatenate(earlier_segments + [segment_own], axis=0)
    key_span = (reach_back + 1) * local_rows
    key_heads = all_pairs[:, :model_width].reshape(key_span, HEADS, HEAD_DIM)
    value_heads = all_pairs[:, model_width:].reshape(key_span, HEADS, HEAD_DIM)
    query_pos = ctx_index * local_rows + jnp.arange(local_rows, dtype=jnp.int32)
    key_pos = (ctx_index - reach_back) * local_rows + jnp.arange(key_span, dtype=jnp.int32)
    allowed = (
        (key_pos[None, :] <= query_pos[:, None])
        & (query_pos[:, None] - key_pos[None, :] < WIN)
        & (key_pos[None, :] >= 0)
        & (segment_own[:, None] == all_segments[None, :])
    )
    scores = window_scores(queries, key_heads, allowed, score_scale)
    largest = jnp.max(scores, axis=-1, keepdims=True)
    exponent = jnp.exp(scores - largest)
    row_total = jnp.sum(exponent, axis=-1, keepdims=True)
    log_total = largest + jnp.log(row_total)
    weights_low = (exponent / row_total).astype(bfloat)
    attended = (
        jnp.einsum("hqk,khd->qhd", weights_low, value_heads, preferred_element_type=single)
        .reshape(local_rows, model_width)
        .astype(bfloat)
    )
    hidden_state = input_rows + jnp.dot(attended, full_out, preferred_element_type=single)
    scale_two = rms_scale(hidden_state)
    normed_two = (hidden_state * scale_two * gain_two).astype(bfloat)
    logits = jnp.dot(normed_two, full_router, preferred_element_type=single)
    expert_ids = jnp.arange(ctx_count, dtype=jnp.int32)
    hits = route_own[:, :, None] == expert_ids[None, None, :]
    picked = hits.astype(single)
    chosen = jnp.sum(logits[:, None, :] * picked, axis=-1)
    gate_weights = jax.nn.softmax(chosen, axis=-1)
    member = jnp.sum(hits.astype(jnp.int32), axis=1)
    ranking = jnp.cumsum(member, axis=0, dtype=jnp.int32) - 1
    slot_ids = jnp.arange(capacity, dtype=jnp.int32)
    placed_mask = (member[:, :, None] > 0) & (ranking[:, :, None] == slot_ids[None, None, :])
    selector = (
        (hits[:, :, :, None] & placed_mask[:, None, :, :])
        .astype(bfloat)
        .reshape(local_rows, TOPK, ctx_count * capacity)
    )
    outgoing = jnp.einsum(
        "tec,td->ecd", placed_mask.astype(bfloat), normed_two, preferred_element_type=single
    ).astype(bfloat)
    incoming = lax.all_to_all(outgoing, "ctx", split_axis=0, concat_axis=0, tiled=True)
    expert_rows = incoming.reshape(ctx_count * capacity, model_width)
    gate_up = jnp.dot(expert_rows, expert_up, preferred_element_type=single)
    hidden_width = gate_up.shape[1] // 2
    expert_gate = gate_up[:, :hidden_width]
    expert_lift = gate_up[:, hidden_width:]
    expert_act = jax.nn.silu(expert_gate)
    expert_hidden = (expert_act * expert_lift).astype(bfloat)
    expert_result = (
        jnp.dot(expert_hidden, expert_back, preferred_element_type=single)
        .astype(bfloat)
        .reshape(ctx_count, capacity, model_width)
    )
    returned = lax.all_to_all(expert_result, "ctx", split_axis=0, concat_axis=0, tiled=True)
    slot_values = jnp.einsum(
        "tks,sd->tkd",
        selector,
        returned.reshape(ctx_count * capacity, model_width),
        preferred_element_type=single,
    )
    mixture = jnp.sum(gate_weights[:, :, None] * slot_values, axis=1)
    shared_both = jnp.dot(normed_two, full_shared_in, preferred_element_type=single)
    shared_gate = shared_both[:, :hidden_width]
    shared_lift = shared_both[:, hidden_width:]
    shared_act = jax.nn.silu(shared_gate)
    shared_hidden = (shared_act * shared_lift).astype(bfloat)
    shared_result = jnp.dot(shared_hidden, full_shared_down, preferred_element_type=single)
    mixed = (hidden_state + mixture + shared_result).astype(bfloat)[None]
    grad_rows = cotangent[0].astype(single)
    grad_low = grad_rows.astype(bfloat)
    grad_shared_down = jnp.dot(shared_hidden.T, grad_low, preferred_element_type=single)
    dshared_hidden = jnp.dot(grad_low, full_shared_down.T, preferred_element_type=single)
    dshared_both = jnp.concatenate(
        [dshared_hidden * shared_lift * silu_slope(shared_gate), dshared_hidden * shared_act],
        axis=1,
    ).astype(bfloat)
    grad_shared_in = jnp.dot(normed_two.T, dshared_both, preferred_element_type=single)
    dnormed_two = jnp.dot(dshared_both, full_shared_in.T, preferred_element_type=single)
    dgates = jnp.sum(grad_rows[:, None, :] * slot_values, axis=-1)
    dslot_low = (gate_weights[:, :, None] * grad_rows[:, None, :]).astype(bfloat)
    slot_grads = (
        jnp.einsum("tks,tkd->sd", selector, dslot_low, preferred_element_type=single)
        .astype(bfloat)
        .reshape(ctx_count, capacity, model_width)
    )
    grad_incoming = lax.all_to_all(slot_grads, "ctx", split_axis=0, concat_axis=0, tiled=True)
    dexpert_result = grad_incoming.reshape(ctx_count * capacity, model_width)
    grad_expert_back = jnp.dot(expert_hidden.T, dexpert_result, preferred_element_type=single)
    dexpert_hidden = jnp.dot(dexpert_result, expert_back.T, preferred_element_type=single)
    dgate_up = jnp.concatenate(
        [dexpert_hidden * expert_lift * silu_slope(expert_gate), dexpert_hidden * expert_act],
        axis=1,
    ).astype(bfloat)
    grad_expert_up = jnp.dot(expert_rows.T, dgate_up, preferred_element_type=single)
    dexpert_rows = (
        jnp.dot(dgate_up, expert_up.T, preferred_element_type=single)
        .astype(bfloat)
        .reshape(ctx_count, capacity, model_width)
    )
    grad_returned = lax.all_to_all(dexpert_rows, "ctx", split_axis=0, concat_axis=0, tiled=True)
    dnormed_two = dnormed_two + jnp.einsum(
        "tks,sd->td",
        selector,
        grad_returned.reshape(ctx_count * capacity, model_width),
        preferred_element_type=single,
    )
    dchosen = gate_weights * (dgates - jnp.sum(gate_weights * dgates, axis=-1, keepdims=True))
    dlogits = jnp.sum(dchosen[:, :, None] * picked, axis=1).astype(bfloat)
    grad_router = jnp.dot(normed_two.T, dlogits, preferred_element_type=single)
    dnormed_two = dnormed_two + jnp.dot(dlogits, full_router.T, preferred_element_type=single)
    dhidden_norm, grad_gain_two = norm_back(dnormed_two, hidden_state, scale_two, gain_two)
    dhidden = grad_rows + dhidden_norm
    dhidden_low = dhidden.astype(bfloat)
    grad_out = jnp.dot(attended.T, dhidden_low, preferred_element_type=single)
    dattended = (
        jnp.dot(dhidden_low, full_out.T, preferred_element_type=single)
        .astype(bfloat)
        .reshape(local_rows, HEADS, HEAD_DIM)
    )
    probs = jnp.exp(window_scores(queries, key_heads, allowed, score_scale) - log_total)
    probs_low = probs.astype(bfloat)
    dprobs = jnp.einsum("qhd,khd->hqk", dattended, value_heads, preferred_element_type=single)
    dscores = (probs * (dprobs - jnp.sum(probs * dprobs, axis=-1, keepdims=True))).astype(bfloat)
    dqueries = (
        jnp.einsum("hqk,khd->qhd", dscores, key_heads, preferred_element_type=single) * score_scale
    )
    dkeys = (
        jnp.einsum("hqk,qhd->khd", dscores, queries, preferred_element_type=single) * score_scale
    )
    dvalues = jnp.einsum("hqk,qhd->khd", probs_low, dattended, preferred_element_type=single)
    dpairs = jnp.concatenate(
        [dkeys.reshape(key_span, model_width), dvalues.reshape(key_span, model_width)], axis=1
    )
    pair_total = dpairs[reach_back * local_rows :]
    for distance in range(1, reach_back + 1):
        lower_edge = (reach_back - distance) * local_rows
        block_grads = dpairs[lower_edge : lower_edge + local_rows]
        pair_total = pair_total + shifted(
            block_grads.astype(jnp.bfloat16), "ctx", -distance
        ).astype(block_grads.dtype)
    dquery_pre = rotate_back(dqueries, cosine_table, sine_table).reshape(local_rows, model_width)
    dkey_pre = rotate_back(
        pair_total[:, :model_width].reshape(local_rows, HEADS, HEAD_DIM), cosine_table, sine_table
    ).reshape(local_rows, model_width)
    dprojected = jnp.concatenate(
        [dquery_pre, dkey_pre, pair_total[:, model_width:]], axis=1
    ).astype(bfloat)
    grad_qkv = jnp.dot(first_normalized.T, dprojected, preferred_element_type=single)
    dnormed_one = jnp.dot(dprojected, full_qkv.T, preferred_element_type=single)
    dinput_norm, grad_gain_one = norm_back(dnormed_one, input_rows, scale_one, gain_one)
    input_grad = (dhidden + dinput_norm)[None]
    dense_grads = (
        lax.psum_scatter(grad_qkv, ("ctx", "fsdp"), scatter_dimension=0, tiled=True),
        lax.psum_scatter(grad_out, ("ctx", "fsdp"), scatter_dimension=0, tiled=True),
        lax.psum_scatter(grad_router, ("ctx", "fsdp"), scatter_dimension=0, tiled=True),
        lax.psum_scatter(grad_shared_in, ("ctx", "fsdp"), scatter_dimension=0, tiled=True),
        lax.psum_scatter(grad_shared_down, ("ctx", "fsdp"), scatter_dimension=0, tiled=True),
        lax.psum_scatter(grad_gain_one, ("ctx", "fsdp"), scatter_dimension=0, tiled=True),
        lax.psum_scatter(grad_gain_two, ("ctx", "fsdp"), scatter_dimension=0, tiled=True),
    )
    expert_grads = (
        lax.psum_scatter(
            grad_expert_up[None].astype(jnp.bfloat16), "fsdp", scatter_dimension=1, tiled=True
        ).astype(jnp.float32),
        lax.psum_scatter(
            grad_expert_back[None].astype(jnp.bfloat16), "fsdp", scatter_dimension=1, tiled=True
        ).astype(jnp.float32),
    )
    return (
        mixed,
        input_grad,
        dense_grads[0],
        dense_grads[1],
        dense_grads[2],
        dense_grads[3],
        dense_grads[4],
        dense_grads[5],
        dense_grads[6],
        expert_grads[0],
        expert_grads[1],
    )


def solution(mesh):
    placed = (
        P("fsdp", "ctx", None),
        P("fsdp", "ctx"),
        P("fsdp", "ctx", None),
        P(("ctx", "fsdp"), None),
        P(("ctx", "fsdp"), None),
        P(("ctx", "fsdp"), None),
        P(("ctx", "fsdp"), None),
        P(("ctx", "fsdp"), None),
        P(("ctx", "fsdp")),
        P(("ctx", "fsdp")),
        P("ctx", "fsdp", None),
        P("ctx", "fsdp", None),
        P("fsdp", "ctx", None),
    )
    return jax.shard_map(
        per_device,
        mesh=mesh,
        in_specs=placed,
        out_specs=(
            P("fsdp", "ctx", None),
            P("fsdp", "ctx", None),
            P(("ctx", "fsdp"), None),
            P(("ctx", "fsdp"), None),
            P(("ctx", "fsdp"), None),
            P(("ctx", "fsdp"), None),
            P(("ctx", "fsdp"), None),
            P(("ctx", "fsdp")),
            P(("ctx", "fsdp")),
            P("ctx", "fsdp", None),
            P("ctx", "fsdp", None),
        ),
        check_vma=False,
    )
```

profile of v0, /device:TPU:1, one launch (start us, length us, event | category | flops | bytes accessed | tf_op | source)
XLA Modules:
  0.0 1369.3 jit_solution(11726569184551943762)
XLA Ops:
  31.8 36.0 %all-gather.2 = bf16[128,6,16]{2,1,0:T(8,128)(2,1)S(1)} all-gather(bf16[1,6,16]{2,1,0:T(8,128)(2,1)} %bitcast.193), channel_id=1, replica_groups=mesh['ctx'=16,'fsdp'=8] {'ctx','fsdp'}, dimensions={0}, use_global_device_ids=true | all-gather | bytes 24768 | tf_op jit(solution)/shard_map/all_gather | solution.py:110
  71.2 63.4 %all-reduce.12 = (bf16[768]{0:T(1024)(128)(2,1)S(1)}, bf16[768]{0:T(1024)(128)(2,1)S(1)}) all-reduce(bf16[768]{0:T(1024)(128)(2,1)S(1)} %dynamic-update-slice, bf16[768]{0:T(1024)(128)(2,1)S(1)} %dynamic-update-slice.1), channel_id=1, replica_groups=mesh['ctx'=16,'fsdp'=8] {'ctx','fsdp'}, use_global_device_ids=true, to_apply=%add | all-reduce | flops 1536 | bytes 6144
  169.8 20.9 %collective-permute-done.1 = bf16[256,1536]{1,0:T(8,128)(2,1)} collective-permute-done((bf16[256,1536]{1,0:T(8,128)(2,1)S(1)}, bf16[256,1536]{1,0:T(8,128)(2,1)}, u32[]{:S(2)}, u32[]{:S(2)}) %collective-permute-start.1) | collective-permute-done | bytes 786464 | tf_op jit(solution)/shard_map/ppermute | solution.py:18
  201.5 8.4 fusion.96
  227.7 31.0 %all-to-all-start = ((bf16[16,48,768]{2,1,0:T(8,128)(2,1)}), bf16[16,48,768]{2,1,0:T(8,128)(2,1)}, u32[]{:S(2)}, u32[]{:S(2)}) async-start(bf16[16,48,768]{2,1,0:T(8,128)(2,1)} %convolution_convert_fusion.2), calls=%async_computation | async-start | bytes 2359296 | tf_op jit(solution)/shard_map/all_to_all | solution.py:201
  261.1 14.1 %all-to-all-done = bf16[16,48,768]{2,1,0:T(8,128)(2,1)} async-done(((bf16[16,48,768]{2,1,0:T(8,128)(2,1)}), bf16[16,48,768]{2,1,0:T(8,128)(2,1)}, u32[]{:S(2)}, u32[]{:S(2)}) %all-to-all-start) | async-done | bytes 1179680 | tf_op jit(solution)/shard_map/all_to_all | solution.py:201
  280.2 10.4 fusion.12
  290.6 9.0 all-to-all-done.2
  299.6 11.1 multiply_convert_fusion.2
  318.6 10.9 fusion.15
  341.5 9.9 fusion.34
  366.6 10.5 reshape.452
  396.7 13.7 multiply_reduce_fusion
  435.3 13.5 collective-permute-start.10
  448.8 10.8 collective-permute-start.9
  459.6 10.8 collective-permute-start.8
  492.0 13.6 collective-permute-done.8
  513.1 371.9 %fusion.92 = (f32[8,2304]{1,0:T(8,128)S(1)}, f32[8,768]{1,0:T(8,128)S(1)}, f32[8,4096]{1,0:T(8,128)S(1)}) fusion(f32[768,2304]{1,0:T(8,128)} %fusion.64, f32[768,768]{1,0:T(8,128)} %fusion.71, f32[768,4096]{1,0:T(8,128)} %fusion.37), kind=kCustom, calls=%all-reduce-scatter.3 | all-reduce-scatter fusion | flops 7340033 | bytes 22249472
  896.8 14.2 %collective-permute-start.66 = (f32[8,768]{1,0:T(8,128)S(1)}, f32[8,768]{1,0:T(8,128)S(1)}, u32[]{:S(2)}, u32[]{:S(2)}) collective-permute-start(f32[8,768]{1,0:T(8,128)S(1)} %get-tuple-element.26), channel_id=1, source_target_pairs={{0,23},{1,24},{2,25},{3,26},{4,27},{5,28},{6,29},{7,30},{8,31},{9,... | collective-permute-start | bytes 73736
  1125.5 10.9 collective-permute-start.86
  1137.6 66.4 %all-reduce.11 = (f32[768,16]{1,0:T(8,128)S(1)}, f32[768]{0:T(1024)S(1)}, f32[768]{0:T(1024)S(1)}) all-reduce(f32[768,16]{1,0:T(8,128)S(1)} %copy-done.35, f32[768]{0:T(1024)S(1)} %get-tuple-element.15, f32[768]{0:T(1024)S(1)} %copy-done.144), channel_id=4, replica_groups=mesh['ctx'=16,'fsdp'=8] {'ctx','fsdp'}, use_global_device_ids=true, to_apply=%region_20.21.clone | all-reduce | flops 13824 | bytes 110592
  1222.9 25.0 %concatenate.52 = f32[262,768]{1,0:T(8,128)S(1)} concatenate(f32[6,768]{1,0:T(8,128)S(1)} %copy-done.121, f32[8,768]{1,0:T(8,128)S(1)} %copy-done.117, f32[8,768]{1,0:T(8,128)S(1)} %copy-done.119, f32[8,768]{1,0:T(8,128)} %copy-done.122, f32[8,768]{1,0:T(8,128)} %copy-done.123, f32[8,768]{1,0:T(8,128)} %copy-done.124, f32[8,768]{1,0:T(8,128)} %copy-done.125, ...), dimensions={0} | concatenate | bytes 1609728
  1248.6 32.6 %concatenate.51 = f32[262,2304]{1,0:T(8,128)S(1)} concatenate(f32[6,2304]{1,0:T(8,128)} %copy-done.86, f32[8,2304]{1,0:T(8,128)} %copy-done.83, f32[8,2304]{1,0:T(8,128)} %copy-done.84, f32[8,2304]{1,0:T(8,128)} %copy-done.85, f32[8,2304]{1,0:T(8,128)} %copy-done.87, f32[8,2304]{1,0:T(8,128)} %copy-done.88, f32[8,2304]{1,0:T(8,128)} %copy-done.89, f32[8,2304]{1,0:T(8,128)} %copy-done.90, ...), dimensions={0} | concatenate | bytes 4829184
  1299.7 56.9 %concatenate.53 = f32[262,4096]{1,0:T(8,128)} concatenate(f32[6,4096]{1,0:T(8,128)S(1)} %copy-done.53, f32[8,4096]{1,0:T(8,128)S(1)} %copy-done.51, f32[8,4096]{1,0:T(8,128)S(1)} %copy-done.55, f32[8,4096]{1,0:T(8,128)S(1)} %copy-done.57, f32[8,4096]{1,0:T(8,128)S(1)} %copy-done.59, f32[8,4096]{1,0:T(8,128)S(1)} %copy-done.61, f32[8,4096]{1,0:T(8,128)} %copy-done.62, ...), dimensions={0} | concatenate | bytes 8585216
  (668 shorter events, 476.1 us)
Async XLA Ops:
  7.2 133.2 %all-gather.17.cloned.1.call-start = ((), (), s32[]{:S(2)}) async-start(), calls=%async_computation.13 | async-start | bytes 4755456 | tf_op jit(solution)/shard_map/all_gather | solution.py:108
  7.9 157.9 %all-gather.19.cloned.1.call-start = ((), (), s32[]{:S(2)}) async-start(), calls=%async_computation.14 | async-start | bytes 1585152 | tf_op jit(solution)/shard_map/all_gather | solution.py:109
  8.7 271.5 %all-gather.11.cloned.1.call-start = ((), (), s32[]{:S(2)}) async-start(), calls=%async_computation.7 | async-start | bytes 7077888 | tf_op jit(solution)/shard_map/all_gather | solution.py:117
  9.4 281.2 %all-gather.13.cloned.1.call-start = ((), (), s32[]{:S(2)}) async-start(), calls=%async_computation.8 | async-start | bytes 3538944 | tf_op jit(solution)/shard_map/all_gather | solution.py:118
  10.0 356.6 %all-gather.21.cloned.1.call-start = ((), (), s32[]{:S(2)}) async-start(), calls=%async_computation.15 | async-start | bytes 8454144 | tf_op jit(solution)/shard_map/all_gather | solution.py:111
  10.6 373.2 %all-gather.15.cloned.1.call-start = ((), (), s32[]{:S(2)}) async-start(), calls=%async_computation.9 | async-start | bytes 3170304 | tf_op jit(solution)/shard_map/all_gather | solution.py:112
  10.6 127.2 %collective-permute-start.4 = (s32[256]{0:T(256)}, s32[256]{0:T(256)S(1)}, u32[]{:S(2)}, u32[]{:S(2)}) collective-permute-start(s32[256]{0:T(256)} %bitcast.187), channel_id=1, source_target_pairs={{0,32},{8,40},{16,48},{24,56},{32,64},{40,72},{48,80},{56,88},{64,... | collective-permute-start | bytes 3080 | tf_op jit(solution)/shard_map/ppermute | solution.py:18
  14.6 124.5 %collective-permute-start.5 = (s32[256]{0:T(256)}, s32[256]{0:T(256)S(1)}, u32[]{:S(2)}, u32[]{:S(2)}) collective-permute-start(s32[256]{0:T(256)} %bitcast.188), channel_id=1, source_target_pairs={{0,24},{8,32},{16,40},{24,48},{32,56},{40,64},{48,72},{56,80},{64,... | collective-permute-start | bytes 3080 | tf_op jit(solution)/shard_map/ppermute | solution.py:18
  20.2 133.0 %collective-permute-start.6 = (s32[256]{0:T(256)}, s32[256]{0:T(256)}, u32[]{:S(2)}, u32[]{:S(2)}) collective-permute-start(s32[256]{0:T(256)} %bitcast.189), channel_id=1, source_target_pairs={{0,16},{8,24},{16,32},{24,40},{32,48},{40,56},{48,64},{56,72},{64,... | collective-permute-start | bytes 3080 | tf_op jit(solution)/shard_map/ppermute | solution.py:18
  23.3 130.6 %collective-permute-start.7 = (s32[256]{0:T(256)}, s32[256]{0:T(256)}, u32[]{:S(2)}, u32[]{:S(2)}) collective-permute-start(s32[256]{0:T(256)} %bitcast.190), channel_id=1, source_target_pairs={{0,8},{8,16},{16,24},{24,32},{32,40},{40,48},{48,56},{56,64},{64,7... | collective-permute-start | bytes 3080 | tf_op jit(solution)/shard_map/ppermute | solution.py:18
  279.7 1078.5 %reduce-scatter.14.cloned.1.call-start = ((), (), s32[]{:S(2)}) async-start(), calls=%async_computation.12 | async-start | bytes 3538944 | tf_op jit(solution)/shard_map/reduce_scatter | solution.py:325
  317.7 1042.4 %reduce-scatter.12.cloned.1.call-start = ((), (), s32[]{:S(2)}) async-start(), calls=%async_computation.11 | async-start | bytes 7077888 | tf_op jit(solution)/shard_map/reduce_scatter | solution.py:322
  363.2 999.4 %reduce-scatter.10.cloned.1.call-start = ((), (), s32[]{:S(2)}) async-start(), calls=%async_computation.10 | async-start | bytes 6340608 | tf_op jit(solution)/shard_map/reduce_scatter | solution.py:317
  434.0 56.1 %collective-permute-start.11 = (bf16[256,1536]{0,1:T(8,128)(2,1)}, bf16[256,1536]{0,1:T(8,128)(2,1)}, u32[]{:S(2)}, u32[]{:S(2)}) collective-permute-start(bf16[256,1536]{0,1:T(8,128)(2,1)} %get-tuple-element.35), channel_id=1, source_target_pairs={{32,0},{40,8},{48,16},{56,24},{64,32},{72,40},{80,48},{88,56},{96,... | collective-permute-start | bytes 2359304 | tf_op jit(solution)/shard_map/ppermute | solution.py:18
  1110.7 93.3 %collective-permute-start.90 = (f32[8,4096]{1,0:T(8,128)S(1)}, f32[8,4096]{1,0:T(8,128)S(1)}, u32[]{:S(2)}, u32[]{:S(2)}) collective-permute-start(f32[8,4096]{1,0:T(8,128)S(1)} %get-tuple-element.27), channel_id=1, source_target_pairs={{0,15},{1,16},{2,17},{3,18},{4,19},{5,20},{6,21},{7,22},{8,23},{9,... | collective-permute-start | bytes 393224
  1116.3 90.7 %collective-permute-start.89 = (f32[8,4096]{1,0:T(8,128)S(1)}, f32[8,4096]{1,0:T(8,128)S(1)}, u32[]{:S(2)}, u32[]{:S(2)}) collective-permute-start(f32[8,4096]{1,0:T(8,128)S(1)} %get-tuple-element.27), channel_id=1, source_target_pairs={{0,14},{1,15},{2,16},{3,17},{4,18},{5,19},{6,20},{7,21},{8,22},{9,... | collective-permute-start | bytes 393224
  1117.6 91.9 %collective-permute-start.88 = (f32[8,4096]{1,0:T(8,128)S(1)}, f32[8,4096]{1,0:T(8,128)S(1)}, u32[]{:S(2)}, u32[]{:S(2)}) collective-permute-start(f32[8,4096]{1,0:T(8,128)S(1)} %get-tuple-element.27), channel_id=1, source_target_pairs={{0,13},{1,14},{2,15},{3,16},{4,17},{5,18},{6,19},{7,20},{8,21},{9,... | collective-permute-start | bytes 393224
  1119.8 93.4 %collective-permute-start.87 = (f32[8,4096]{1,0:T(8,128)S(1)}, f32[8,4096]{1,0:T(8,128)S(1)}, u32[]{:S(2)}, u32[]{:S(2)}) collective-permute-start(f32[8,4096]{1,0:T(8,128)S(1)} %get-tuple-element.27), channel_id=1, source_target_pairs={{0,12},{1,13},{2,14},{3,15},{4,16},{5,17},{6,18},{7,19},{8,20},{9,... | collective-permute-start | bytes 393224
  1125.5 91.1 %collective-permute-start.86 = (f32[8,4096]{1,0:T(8,128)S(1)}, f32[8,4096]{1,0:T(8,128)}, u32[]{:S(2)}, u32[]{:S(2)}) collective-permute-start(f32[8,4096]{1,0:T(8,128)S(1)} %get-tuple-element.27), channel_id=1, source_target_pairs={{0,11},{1,12},{2,13},{3,14},{4,15},{5,16},{6,17},{7,18},{8,19},{9,... | collective-permute-start | bytes 393224
  1204.0 77.2 %collective-permute-start.85 = (f32[8,4096]{1,0:T(8,128)S(1)}, f32[8,4096]{1,0:T(8,128)}, u32[]{:S(2)}, u32[]{:S(2)}) collective-permute-start(f32[8,4096]{1,0:T(8,128)S(1)} %get-tuple-element.27), channel_id=1, source_target_pairs={{0,10},{1,11},{2,12},{3,13},{4,14},{5,15},{6,16},{7,17},{8,18},{9,... | collective-permute-start | bytes 393224
  1207.0 76.4 %collective-permute-start.84 = (f32[8,4096]{1,0:T(8,128)S(1)}, f32[8,4096]{1,0:T(8,128)}, u32[]{:S(2)}, u32[]{:S(2)}) collective-permute-start(f32[8,4096]{1,0:T(8,128)S(1)} %get-tuple-element.27), channel_id=1, source_target_pairs={{0,9},{1,10},{2,11},{3,12},{4,13},{5,14},{6,15},{7,16},{8,17},{9,1... | collective-permute-start | bytes 393224
  1209.5 77.7 %collective-permute-start.83 = (f32[8,4096]{1,0:T(8,128)S(1)}, f32[8,4096]{1,0:T(8,128)}, u32[]{:S(2)}, u32[]{:S(2)}) collective-permute-start(f32[8,4096]{1,0:T(8,128)S(1)} %get-tuple-element.27), channel_id=1, source_target_pairs={{0,8},{1,9},{2,10},{3,11},{4,12},{5,13},{6,14},{7,15},{8,16},{9,17... | collective-permute-start | bytes 393224
  1213.2 78.0 %collective-permute-start.82 = (f32[8,4096]{1,0:T(8,128)S(1)}, f32[8,4096]{1,0:T(8,128)}, u32[]{:S(2)}, u32[]{:S(2)}) collective-permute-start(f32[8,4096]{1,0:T(8,128)S(1)} %get-tuple-element.27), channel_id=1, source_target_pairs={{0,7},{1,8},{2,9},{3,10},{4,11},{5,12},{6,13},{7,14},{8,15},{9,16}... | collective-permute-start | bytes 393224
  1216.6 76.9 %collective-permute-start.81 = (f32[8,4096]{1,0:T(8,128)S(1)}, f32[8,4096]{1,0:T(8,128)}, u32[]{:S(2)}, u32[]{:S(2)}) collective-permute-start(f32[8,4096]{1,0:T(8,128)S(1)} %get-tuple-element.27), channel_id=1, source_target_pairs={{0,6},{1,7},{2,8},{3,9},{4,10},{5,11},{6,12},{7,13},{8,14},{9,15},... | collective-permute-start | bytes 393224
  (252 other events, 8156.8 us)
Sparse Core Ops, SparseCore 0:
  11.1 70.7 all-gather.16
  84.7 61.6 all-gather.18
  148.1 38.3 all-gather.10
  188.0 27.8 all-gather.12
  218.7 82.5 all-gather.20
  304.3 66.5 all-gather.14
  373.2 34.4 reduce-scatter.13
  410.1 43.6 reduce-scatter.11
  480.8 220.4 reduce-scatter.9
where the time goes:
time: 1390 us; the launch traced here: 1370 us
  blocking collectives  538 us (39%)
  starting transfers between devices  386 us (28%)
  local copies, waits for them, and re-layouts  173 us (12%)
  matrix products  146 us (11%)
  waiting for transfers between devices  71.4 us (5%)
  other arithmetic  37.6 us (3%)
  between operations  17.5 us (1%)
    unnamed x3, blocking collectives  502 us
    unnamed x96, starting transfers between devices  273 us
    unnamed x338, local copies, waits for them, and re-layouts  162 us
    ppermute x12, starting transfers between devices, shifted(): lax.ppermute(value, axis, [(source, source + steps) for source in range(l...  65.5 us
    ppermute x12, waiting for transfers between devices, shifted(): lax.ppermute(value, axis, [(source, source + steps) for source in range(l...  37.3 us
    all_gather x1, blocking collectives, per_device(): lax.all_gather(w_router, ('ctx', 'fsdp'), axis=0, tiled=True)  36 us
    all_to_all x1, starting transfers between devices, per_device(): lax.all_to_all(outgoing, 'ctx', split_axis=0, concat_axis=0, tiled=True)  31 us
  transfers between devices with their start and end apart: 121, of which 10 were waited for; matrix products, arithmetic and copies ran while one was open for 52% of the time, Pallas kernels for 0%

commit v1 on v0

--- a/solution.py
+++ b/solution.py
@@ -78,6 +78,15 @@
         * score_scale
     )
     return jnp.where(allowed[None], scores, -1e30)
+
+
+def sum_to_owners(grads, rows):
+    low = grads.astype(jnp.bfloat16).reshape(
+        lax.axis_size("ctx"), lax.axis_size("fsdp"), rows, grads.shape[-1]
+    )
+    part = lax.psum_scatter(low.transpose(1, 0, 2, 3), "fsdp", scatter_dimension=0)
+    pieces = lax.all_to_all(part, "ctx", split_axis=0, concat_axis=0, tiled=True)
+    return jnp.sum(pieces.astype(jnp.float32), axis=0)
 
 
 def per_device(
@@ -104,21 +113,52 @@
     score_scale = HEAD_DIM ** (-0.5)
     bfloat = jnp.bfloat16
     single = jnp.float32
-    dense_full = (
-        lax.all_gather(w_qkv, ("ctx", "fsdp"), axis=0, tiled=True),
-        lax.all_gather(w_out, ("ctx", "fsdp"), axis=0, tiled=True),
-        lax.all_gather(w_router, ("ctx", "fsdp"), axis=0, tiled=True),
-        lax.all_gather(shared_in, ("ctx", "fsdp"), axis=0, tiled=True),
-        lax.all_gather(shared_down, ("ctx", "fsdp"), axis=0, tiled=True),
-        lax.all_gather(attn_gain, ("ctx", "fsdp"), axis=0, tiled=True),
-        lax.all_gather(ffn_gain, ("ctx", "fsdp"), axis=0, tiled=True),
-    )
+    rows_own = w_qkv.shape[0]
+    rows_down = shared_down.shape[0]
+    small = jnp.concatenate(
+        [
+            w_router,
+            attn_gain[:, None],
+            ffn_gain[:, None],
+            jnp.zeros((rows_own, 128 - w_router.shape[1] - 2), w_router.dtype),
+        ],
+        axis=1,
+    )
+    packed = jnp.pad(
+        jnp.concatenate([w_qkv, w_out, shared_in, small], axis=1), ((0, 8 - rows_own), (0, 0))
+    )
+    packed = jnp.concatenate([packed, shared_down[:8], shared_down[8:]], axis=1)
+    gathered = lax.all_gather(packed, ("ctx", "fsdp"), axis=0, tiled=True)
+    device_count = ctx_count * lax.axis_size("fsdp")
+    gathered = gathered.reshape(device_count, 8, gathered.shape[1])
+
+    def columns(start, width):
+        return gathered[:, :rows_own, start : start + width].reshape(
+            device_count * rows_own, width
+        )
+
+    place = 0
+    full_qkv = columns(place, w_qkv.shape[1])
+    place += w_qkv.shape[1]
+    full_out = columns(place, w_out.shape[1])
+    place += w_out.shape[1]
+    full_shared_in = columns(place, shared_in.shape[1])
+    place += shared_in.shape[1]
+    full_small = columns(place, 128)
+    place += 128
+    full_shared_down = (
+        gathered[:, :, place:]
+        .reshape(device_count, 8, 2, model_width)
+        .transpose(0, 2, 1, 3)
+        .reshape(device_count * rows_down, model_width)
+    )
+    expert_count = w_router.shape[1]
+    full_router = full_small[:, :expert_count]
+    gain_attn = full_small[:, expert_count]
+    gain_ffn = full_small[:, expert_count + 1]
     expert_full = (
         lax.all_gather(expert_in, "fsdp", axis=1, tiled=True),
         lax.all_gather(expert_down, "fsdp", axis=1, tiled=True),
-    )
-    full_qkv, full_out, full_router, full_shared_in, full_shared_down, gain_attn, gain_ffn = (
-        dense_full
     )
     expert_up = expert_full[0][0]
     expert_back = expert_full[1][0]
@@ -127,37 +167,37 @@
     route_own = routes[0]
     gain_one = gain_attn.astype(single)
     gain_two = gain_ffn.astype(single)
-    scale_one = rms_scale(input_rows)
-    first_normalized = (input_rows * scale_one * gain_one).astype(bfloat)
-    projected_output = jnp.dot(first_normalized, full_qkv, preferred_element_type=single)
-    cosine_table, sine_table = rotary_table(local_rows, ctx_index * local_rows, HEAD_DIM)
-    queries = rotate(
-        projected_output[:, :model_width].reshape(local_rows, HEADS, HEAD_DIM),
-        cosine_table,
-        sine_table,
-    ).astype(bfloat)
-    key_own = (
-        rotate(
-            projected_output[:, model_width : 2 * model_width].reshape(local_rows, HEADS, HEAD_DIM),
-            cosine_table,
-            sine_table,
-        )
-        .astype(bfloat)
-        .reshape(local_rows, model_width)
-    )
-    value_own = projected_output[:, 2 * model_width :].astype(bfloat)
-    key_value = jnp.concatenate([key_own, value_own], axis=1)
-    earlier_pairs = []
+    earlier_rows = []
     earlier_segments = []
     for distance in range(reach_back, 0, -1):
-        moved_pair, moved_segment = shifted((key_value, segment_own), "ctx", distance)
-        earlier_pairs.append(moved_pair)
+        moved_rows, moved_segment = shifted((tokens[0], segment_own), "ctx", distance)
+        earlier_rows.append(moved_rows)
         earlier_segments.append(moved_segment)
-    all_pairs = jnp.concatenate(earlier_pairs + [key_value], axis=0)
+    span_rows = jnp.concatenate(earlier_rows + [tokens[0]], axis=0).astype(single)
     all_segments = jnp.concatenate(earlier_segments + [segment_own], axis=0)
+    span_scale = rms_scale(span_rows)
+    span_normalized = (span_rows * span_scale * gain_one).astype(bfloat)
+    scale_one = span_scale[reach_back * local_rows :]
+    first_normalized = span_normalized[reach_back * local_rows :]
     key_span = (reach_back + 1) * local_rows
-    key_heads = all_pairs[:, :model_width].reshape(key_span, HEADS, HEAD_DIM)
-    value_heads = all_pairs[:, model_width:].reshape(key_span, HEADS, HEAD_DIM)
+    queries_flat = jnp.dot(
+        first_normalized, full_qkv[:, :model_width], preferred_element_type=single
+    )
+    pairs_flat = jnp.dot(
+        span_normalized, full_qkv[:, model_width:], preferred_element_type=single
+    )
+    span_cosine, span_sine = rotary_table(
+        key_span, (ctx_index - reach_back) * local_rows, HEAD_DIM
+    )
+    cosine_table = span_cosine[reach_back * local_rows :]
+    sine_table = span_sine[reach_back * local_rows :]
+    queries = rotate(
+        queries_flat.reshape(local_rows, HEADS, HEAD_DIM), cosine_table, sine_table
+    ).astype(bfloat)
+    key_heads = rotate(
+        pairs_flat[:, :model_width].reshape(key_span, HEADS, HEAD_DIM), span_cosine, span_sine
+    ).astype(bfloat)
+    value_heads = pairs_flat[:, model_width:].astype(bfloat).reshape(key_span, HEADS, HEAD_DIM)
     query_pos = ctx_index * local_rows + jnp.arange(local_rows, dtype=jnp.int32)
     key_pos = (ctx_index - reach_back) * local_rows + jnp.arange(key_span, dtype=jnp.int32)
     allowed = (
@@ -198,7 +238,16 @@
     outgoing = jnp.einsum(
         "tec,td->ecd", placed_mask.astype(bfloat), normed_two, preferred_element_type=single
     ).astype(bfloat)
+    grad_rows = cotangent[0].astype(single)
+    grad_low = grad_rows.astype(bfloat)
+    dslot_low = (gate_weights[:, :, None] * grad_rows[:, None, :]).astype(bfloat)
+    slot_grads = (
+        jnp.einsum("tks,tkd->sd", selector, dslot_low, preferred_element_type=single)
+        .astype(bfloat)
+        .reshape(ctx_count, capacity, model_width)
+    )
     incoming = lax.all_to_all(outgoing, "ctx", split_axis=0, concat_axis=0, tiled=True)
+    grad_incoming = lax.all_to_all(slot_grads, "ctx", split_axis=0, concat_axis=0, tiled=True)
     expert_rows = incoming.reshape(ctx_count * capacity, model_width)
     gate_up = jnp.dot(expert_rows, expert_up, preferred_element_type=single)
     hidden_width = gate_up.shape[1] // 2
@@ -226,8 +275,6 @@
     shared_hidden = (shared_act * shared_lift).astype(bfloat)
     shared_result = jnp.dot(shared_hidden, full_shared_down, preferred_element_type=single)
     mixed = (hidden_state + mixture + shared_result).astype(bfloat)[None]
-    grad_rows = cotangent[0].astype(single)
-    grad_low = grad_rows.astype(bfloat)
     grad_shared_down = jnp.dot(shared_hidden.T, grad_low, preferred_element_type=single)
     dshared_hidden = jnp.dot(grad_low, full_shared_down.T, preferred_element_type=single)
     dshared_both = jnp.concatenate(
@@ -237,13 +284,6 @@
     grad_shared_in = jnp.dot(normed_two.T, dshared_both, preferred_element_type=single)
     dnormed_two = jnp.dot(dshared_both, full_shared_in.T, preferred_element_type=single)
     dgates = jnp.sum(grad_rows[:, None, :] * slot_values, axis=-1)
-    dslot_low = (gate_weights[:, :, None] * grad_rows[:, None, :]).astype(bfloat)
-    slot_grads = (
-        jnp.einsum("tks,tkd->sd", selector, dslot_low, preferred_element_type=single)
-        .astype(bfloat)
-        .reshape(ctx_count, capacity, model_width)
-    )
-    grad_incoming = lax.all_to_all(slot_grads, "ctx", split_axis=0, concat_axis=0, tiled=True)
     dexpert_result = grad_incoming.reshape(ctx_count * capacity, model_width)
     grad_expert_back = jnp.dot(expert_hidden.T, dexpert_result, preferred_element_type=single)
     dexpert_hidden = jnp.dot(dexpert_result, expert_back.T, preferred_element_type=single)
@@ -288,35 +328,58 @@
         jnp.einsum("hqk,qhd->khd", dscores, queries, preferred_element_type=single) * score_scale
     )
     dvalues = jnp.einsum("hqk,qhd->khd", probs_low, dattended, preferred_element_type=single)
+    dquery_low = (
+        rotate_back(dqueries, cosine_table, sine_table)
+        .reshape(local_rows, model_width)
+        .astype(bfloat)
+    )
+    dkey_low = (
+        rotate_back(dkeys, span_cosine, span_sine).reshape(key_span, model_width).astype(bfloat)
+    )
     dpairs = jnp.concatenate(
-        [dkeys.reshape(key_span, model_width), dvalues.reshape(key_span, model_width)], axis=1
-    )
-    pair_total = dpairs[reach_back * local_rows :]
+        [dkey_low, dvalues.reshape(key_span, model_width).astype(bfloat)], axis=1
+    )
+    grad_qkv = jnp.concatenate(
+        [
+            jnp.dot(first_normalized.T, dquery_low, preferred_element_type=single),
+            jnp.dot(span_normalized.T, dpairs, preferred_element_type=single),
+        ],
+        axis=1,
+    )
+    dspan_one = jnp.dot(dpairs, full_qkv[:, model_width:].T, preferred_element_type=single)
+    dnormed_one = dspan_one[reach_back * local_rows :] + jnp.dot(
+        dquery_low, full_qkv[:, :model_width].T, preferred_element_type=single
+    )
     for distance in range(1, reach_back + 1):
         lower_edge = (reach_back - distance) * local_rows
-        block_grads = dpairs[lower_edge : lower_edge + local_rows]
-        pair_total = pair_total + shifted(
+        block_grads = dspan_one[lower_edge : lower_edge + local_rows]
+        dnormed_one = dnormed_one + shifted(
             block_grads.astype(jnp.bfloat16), "ctx", -distance
-        ).astype(block_grads.dtype)
-    dquery_pre = rotate_back(dqueries, cosine_table, sine_table).reshape(local_rows, model_width)
-    dkey_pre = rotate_back(
-        pair_total[:, :model_width].reshape(local_rows, HEADS, HEAD_DIM), cosine_table, sine_table
-    ).reshape(local_rows, model_width)
-    dprojected = jnp.concatenate(
-        [dquery_pre, dkey_pre, pair_total[:, model_width:]], axis=1
-    ).astype(bfloat)
-    grad_qkv = jnp.dot(first_normalized.T, dprojected, preferred_element_type=single)
-    dnormed_one = jnp.dot(dprojected, full_qkv.T, preferred_element_type=single)
+        ).astype(single)
     dinput_norm, grad_gain_one = norm_back(dnormed_one, input_rows, scale_one, gain_one)
     input_grad = (dhidden + dinput_norm)[None]
+    grad_small = jnp.concatenate(
+        [
+            grad_router,
+            grad_gain_one[:, None],
+            grad_gain_two[:, None],
+            jnp.zeros((model_width, 128 - expert_count - 2), single),
+        ],
+        axis=1,
+    )
+    early_grads = sum_to_owners(grad_shared_in, rows_own)
+    down_grads = sum_to_owners(grad_shared_down, rows_down)
+    late_grads = sum_to_owners(jnp.concatenate([grad_qkv, grad_out, grad_small], axis=1), rows_own)
+    qkv_width = grad_qkv.shape[1]
+    last = qkv_width + model_width
     dense_grads = (
-        lax.psum_scatter(grad_qkv, ("ctx", "fsdp"), scatter_dimension=0, tiled=True),
-        lax.psum_scatter(grad_out, ("ctx", "fsdp"), scatter_dimension=0, tiled=True),
-        lax.psum_scatter(grad_router, ("ctx", "fsdp"), scatter_dimension=0, tiled=True),
-        lax.psum_scatter(grad_shared_in, ("ctx", "fsdp"), scatter_dimension=0, tiled=True),
-        lax.psum_scatter(grad_shared_down, ("ctx", "fsdp"), scatter_dimension=0, tiled=True),
-        lax.psum_scatter(grad_gain_one, ("ctx", "fsdp"), scatter_dimension=0, tiled=True),
-        lax.psum_scatter(grad_gain_two, ("ctx", "fsdp"), scatter_dimension=0, tiled=True),
+        late_grads[:, :qkv_width],
+        late_grads[:, qkv_width:last],
+        late_grads[:, last : last + expert_count],
+        early_grads,
+        down_grads,
+        late_grads[:, last + expert_count],
+        late_grads[:, last + expert_count + 1],
     )
     expert_grads = (
         lax.psum_scatter(

time: 1390 us -> 620 us (0.45)
  blocking collectives: 538 us -> 0 us
  starting transfers between devices: 386 us -> 84.7 us
  waiting for transfers between devices: 71.4 us -> 176 us
  local copies, waits for them, and re-layouts: 173 us -> 130 us
    unnamed x3 -> x0, blocking collectives: 502 us -> none
    unnamed x96 -> x1, starting transfers between devices: 273 us -> 0.04 us
    unnamed x338 -> x161, local copies, waits for them, and re-layouts: 162 us -> 10.4 us
    all_gather x4 -> x1, waiting for transfers between devices: 0.03 us -> 54.5 us  [per_device(): gathered = lax.all_gather(packed, ('ctx', 'fsdp'), axis=0, tiled=True)]
    reduce_scatter x1, waiting for transfers between devices: 0.01 us -> 40.4 us  [per_device(): lax.psum_scatter(grad_expert_up[None].astype(jnp.bfloat16), 'fsdp', scatt...]
    all_gather x1 -> x0, blocking collectives: 36 us -> none  [per_device(): lax.all_gather(w_router, ('ctx', 'fsdp'), axis=0, tiled=True)]
    ppermute x12, starting transfers between devices: 65.5 us -> 32.3 us  [shifted(): lax.ppermute(value, axis, [(source, source + steps) for source in range(l...]
    all_to_all x0 -> x3, starting transfers between devices: none -> 28.9 us  [sum_to_owners(): lax.all_to_all(part, 'ctx', split_axis=0, concat_axis=0, tiled=True)]
  transfers between devices with their start and end apart: 121 -> 27, of which waited for: 10 -> 13; matrix products, arithmetic and copies ran while one was open for 52% -> 52% of each run, Pallas kernels for 0% -> 0%
where the time goes in v1:
time: 620 us; the launch traced here: 612 us
  waiting for transfers between devices  176 us (28%)
  matrix products  158 us (25%)
  local copies, waits for them, and re-layouts  130 us (21%)
  starting transfers between devices  84.7 us (14%)
  other arithmetic  47.5 us (8%)
  between operations  15.7 us (3%)
    all_gather x1, waiting for transfers between devices, per_device(): gathered = lax.all_gather(packed, ('ctx', 'fsdp'), axis=0, tiled=True)  54.5 us
    reduce_scatter x1, waiting for transfers between devices, per_device(): lax.psum_scatter(grad_expert_up[None].astype(jnp.bfloat16), 'fsdp', scatt...  40.4 us
    ppermute x12, starting transfers between devices, shifted(): lax.ppermute(value, axis, [(source, source + steps) for source in range(l...  32.3 us
    all_to_all x3, starting transfers between devices, sum_to_owners(): lax.all_to_all(part, 'ctx', split_axis=0, concat_axis=0, tiled=True)  28.9 us
    reduce_scatter x1, waiting for transfers between devices, per_device(): lax.psum_scatter(grad_expert_back[None].astype(jnp.bfloat16), 'fsdp', sca...  24.5 us
    reduce_scatter x2, waiting for transfers between devices, sum_to_owners(): lax.psum_scatter(low.transpose(1, 0, 2, 3), 'fsdp', scatter_dimension=0)  17.8 us
    transpose x2, local copies, waits for them, and re-layouts, sum_to_owners(): low.transpose(1, 0, 2, 3)  17.8 us
    reshape x4, local copies, waits for them, and re-layouts, columns(): gathered[:, :rows_own, start:start + width]  17.6 us
  transfers between devices with their start and end apart: 27, of which 13 were waited for; matrix products, arithmetic and copies ran while one was open for 52% of the time, Pallas kernels for 0%

profile of v1, /device:TPU:1, one launch (start us, length us, event | category | flops | bytes accessed | tf_op | source)
XLA Modules:
  0.0 611.7 jit_solution(2793606410231011098)
XLA Ops:
  54.6 54.5 %all-gather.4.cloned.1.call-done = bf16[1024,8832]{1,0:T(8,128)(2,1)} async-done(((bf16[8,8832]{1,0:T(8,128)(2,1)}), bf16[1024,8832]{1,0:T(8,128)(2,1)}) %all-gather.4.cloned.1.call-update) | async-done | bytes 18087952 | tf_op jit(solution)/shard_map/all_gather | solution.py:131
  121.5 7.9 %slice.201 = bf16[128,6,4096]{2,1,0:T(8,128)(2,1)} slice(bf16[128,8,8832]{2,1,0:T(8,128)(2,1)} %bitcast.188), slice={[0:128], [0:6], [3072:7168]} | slice | bytes 12582912 | tf_op jit(solution)/shard_map/slice | solution.py:136
  132.1 6.9 %reshape.482 = bf16[768,2304]{1,0:T(8,128)(2,1)} reshape(bf16[128,6,2304]{2,1,0:T(8,128)(2,1)} %slice.183) | data formatting | bytes 7077888 | tf_op jit(solution)/shard_map/reshape | solution.py:136
  150.9 10.2 %reshape.491 = bf16[768,4096]{1,0:T(8,128)(2,1)} reshape(bf16[128,6,4096]{2,1,0:T(8,128)(2,1)} %slice.201) | data formatting | bytes 12582912 | tf_op jit(solution)/shard_map/reshape | solution.py:136
  175.5 8.8 %fusion.98 = (f32[12,256]{1,0:T(8,128)S(1)}, f32[12,256,1280]{2,1,0:T(8,128)}) fusion(bf16[1280,12,32]{0,2,1:T(8,128)(2,1)} %get-tuple-element.30, bf16[1280,12,32]{0,2,1:T(8,128)(2,1)} %get-tuple-element.29, bf16[256,12,32]{0,2,1:T(8,128)(2,1)S(1)} %get-tuple-element.39, bf16[256,12,32]{0,2,1:T(8,128)(2,1)S(1)} %get-tuple-element.38, ...), kind=kOutput, calls=%fused_computation.204 | convolution fusion | flops 519828480 | bytes 18427904 | tf_op jit(solution)/shard_map/qhd,khd->hqk/dot_general | solution.py:77
  184.3 7.8 %fusion = f32[12,256]{1,0:T(8,128)S(1)} fusion(f32[12,256,1280]{2,1,0:T(8,128)} %get-tuple-element.47, f32[12,256]{1,0:T(8,128)S(1)} %get-tuple-element.46), kind=kLoop, calls=%fused_computation.6 | loop fusion | flops 7861248 | bytes 15753216 | tf_op jit(solution)/shard_map/reduce_sum | solution.py:212
  192.1 7.1 %fusion.46 = bf16[12,64,256]{2,1,0:T(8,128)(2,1)S(1)} fusion(bf16[1280,12,64]{0,2,1:T(8,128)(2,1)S(1)} %bitcast.190, f32[12,256,1280]{2,1,0:T(8,128)} %get-tuple-element.47, f32[12,256]{1,0:T(8,128)S(1)} %fusion, f32[12,256]{1,0:T(8,128)S(1)} %get-tuple-element.46), kind=kOutput, calls=%fused_computation.95 | convolution fusion | flops 515309568 | bytes 18112512 | tf_op jit(solution)/shard_map/hqk,khd->qhd/dot_general | solution.py:216
  234.4 7.1 %all-to-all-start.2 = ((bf16[16,48,768]{2,1,0:T(8,128)(2,1)}), bf16[16,48,768]{2,1,0:T(8,128)(2,1)}, u32[]{:S(2)}, u32[]{:S(2)}) async-start(bf16[16,48,768]{2,1,0:T(8,128)(2,1)} %bitcast.209), calls=%async_computation.2 | async-start | bytes 2359296 | tf_op jit(solution)/shard_map/all_to_all | solution.py:250
  241.5 10.2 %fusion.8 = f32[768,4096]{1,0:T(8,128)} fusion(bf16[768,768]{1,0:T(8,128)(2,1)} %bitcast.14, bf16[1,768,4096]{2,1,0:T(8,128)(2,1)} %all-gather.6.cloned.1.call-done), kind=kOutput, calls=%fused_computation.16 | convolution fusion | flops 4831838208 | bytes 20054016 | tf_op jit(solution)/shard_map/dot_general | solution.py:252
  258.1 11.2 %multiply_convert_fusion.2 = (bf16[768,2048]{1,0:T(8,128)(2,1)}, bf16[768,2048]{1,0:T(8,128)(2,1)}, bf16[768,2048]{1,0:T(8,128)(2,1)S(1)}) fusion(f32[768,4096]{1,0:T(8,128)} %fusion.8, bf16[768,768]{1,0:T(8,128)(2,1)} %bitcast.34, bf16[1,2048,768]{2,1,0:T(8,128)(2,1)} %all-gather.8.cloned.1.call-done), kind=kOutput, calls=%fused_computation.19 | convolution fusion | flops 2439512064 | bytes 26345472 | tf_op jit(solution)/shard_map/dot_general | solution.py:289
  277.4 10.0 %fusion.36 = bf16[768,768]{1,0:T(8,128)(2,1)} fusion(bf16[1,768,4096]{2,1,0:T(8,128)(2,1)} %all-gather.6.cloned.1.call-done, bf16[768,2048]{1,0:T(8,128)(2,1)} %get-tuple-element.23, bf16[768,2048]{1,0:T(8,128)(2,1)} %get-tuple-element.22), kind=kOutput, calls=%fused_computation.76 | convolution fusion | flops 4845010944 | bytes 13762560 | tf_op jit(solution)/shard_map/dot_general | solution.py:296
  302.5 11.0 %all-to-all-done.3 = bf16[16,48,768]{2,1,0:T(8,128)(2,1)} async-done(((bf16[16,48,768]{2,1,0:T(8,128)(2,1)}), bf16[16,48,768]{2,1,0:T(8,128)(2,1)}, u32[]{:S(2)}, u32[]{:S(2)}) %all-to-all-start.3) | async-done | bytes 1179680 | tf_op jit(solution)/shard_map/all_to_all | solution.py:300
  318.4 9.5 %fusion.16 = bf16[12,64,1280]{2,1,0:T(8,128)(2,1)} fusion(bf16[256,12,64]{0,2,1:T(8,128)(2,1)S(1)} %bitcast.192, f32[12,256,1280]{2,1,0:T(8,128)} %get-tuple-element.47, f32[12,256]{1,0:T(8,128)S(1)} %log_add_fusion), kind=kOutput, calls=%fused_computation.33 | convolution fusion | flops 512163840 | bytes 18100224 | tf_op jit(solution)/shard_map/hqk,qhd->khd/dot_general | solution.py:330
  327.9 12.4 %multiply_reduce_fusion = (f32[12,256]{1,0:T(8,128)S(1)}, f32[12,256,1280]{2,1,0:T(8,128)}) fusion(f32[12,256,1280]{2,1,0:T(8,128)} %get-tuple-element.47, f32[12,256]{1,0:T(8,128)S(1)} %log_add_fusion, bf16[256,12,64]{0,2,1:T(8,128)(2,1)S(1)} %bitcast.193, bf16[1280,12,64]{0,2,1:T(8,128)(2,1)} %bitcast.191), kind=kOutput, calls=%fused_computation.1 | convolution fusion | flops 515109888 | bytes 33841152 | tf_op jit(solution)/shard_map/qhd,khd->hqk/dot_general | solution.py:322
  340.4 9.9 %multiply_convert_fusion = bf16[12,256,1280]{2,1,0:T(8,128)(2,1)} fusion(f32[12,256,1280]{2,1,0:T(8,128)} %get-tuple-element.52, f32[12,256,1280]{2,1,0:T(8,128)S(1)} %bitcast.180, f32[12,256]{1,0:T(8,128)S(1)} %get-tuple-element.51, f32[12,256]{1,0:T(8,128)S(1)} %log_add_fusion), kind=kLoop, calls=%fused_computation | loop fusion | flops 15728640 | bytes 39346176 | tf_op jit(solution)/shard_map/convert_element_type | solution.py:323
  401.4 10.4 %concatenate.66 = bf16[16,8,6,3200]{3,2,1,0:T(8,128)(2,1)} concatenate(bf16[16,8,6,768]{3,2,1,0:T(8,128)(2,1)} %copy.92, bf16[16,8,6,1536]{3,2,1,0:T(8,128)(2,1)S(1)} %concatenate.62, bf16[16,8,6,768]{3,2,1,0:T(8,128)(2,1)} %copy.93, bf16[16,8,6,16]{3,2,1,0:T(8,128)(2,1)} %concatenate.63, bf16[16,8,6,1]{3,2,1,0:T(8,128)(2,1)} %concatenate.67, bf16[16,8,6,1]{3,2,1,0:T(8,128)(2,1)} %concatenate.68, ...), dimensions={3} | concatenate | bytes 9830400 | tf_op jit(solution)/shard_map/concatenate | solution.py:372
  411.8 7.7 %copy.96 = bf16[8,16,6,3200]{3,1,2,0:T(8,128)(2,1)} copy(bf16[8,16,6,3200]{3,2,0,1:T(8,128)(2,1)} %bitcast.182) | data formatting | bytes 9830400 | tf_op jit(solution)/shard_map/transpose | solution.py:87
  425.6 10.4 %reshape.498 = bf16[16,8,6,4096]{3,2,1,0:T(8,128)(2,1)} reshape(bf16[768,4096]{1,0:T(8,128)(2,1)} %convolution_convert_fusion) | data formatting | bytes 12582912 | tf_op jit(solution)/shard_map/reshape | solution.py:84
  436.0 10.1 %copy.98 = bf16[8,16,6,4096]{3,1,2,0:T(8,128)(2,1)} copy(bf16[8,16,6,4096]{3,2,0,1:T(8,128)(2,1)} %bitcast.181) | data formatting | bytes 12582912 | tf_op jit(solution)/shard_map/transpose | solution.py:87
  455.3 8.5 %fusion.11 = bf16[1,768,4096]{2,1,0:T(8,128)(2,1)} fusion(bf16[768,768]{1,0:T(8,128)(2,1)} %bitcast.14, bf16[768,2048]{1,0:T(8,128)(2,1)} %get-tuple-element.23, bf16[768,2048]{1,0:T(8,128)(2,1)S(1)} %copy-done.71), kind=kOutput, calls=%fused_computation.23 | convolution fusion | flops 4847566848 | bytes 13762560 | tf_op jit(solution)/shard_map/dot_general | solution.py:294
  467.5 18.4 %all-to-all-start.6 = ((bf16[16,16,768]{2,1,0:T(8,128)(2,1)}), bf16[16,16,768]{2,1,0:T(8,128)(2,1)S(1)}, u32[]{:S(2)}, u32[]{:S(2)}) async-start(bf16[16,16,768]{2,1,0:T(8,128)(2,1)} %dynamic-slice_bitcast_fusion), calls=%async_computation.8 | async-start | bytes 786432 | tf_op jit(solution)/shard_map/all_to_all | solution.py:88
  502.3 17.8 %reduce-scatter.10.cloned.1.call-done = bf16[1,16,6,4096]{3,1,2,0:T(8,128)(2,1)} async-done(((bf16[8,16,6,4096]{3,1,2,0:T(8,128)(2,1)}), bf16[1,16,6,4096]{3,1,2,0:T(8,128)(2,1)}) %reduce-scatter.10.cloned.1.call-update) | async-done | bytes 786448 | tf_op jit(solution)/shard_map/reduce_scatter | solution.py:87
  531.6 24.5 %reduce-scatter.14.cloned.1.call-done = bf16[1,256,768]{2,1,0:T(8,128)(2,1)} async-done(((bf16[1,2048,768]{2,1,0:T(8,128)(2,1)}), bf16[1,256,768]{2,1,0:T(8,128)(2,1)}) %reduce-scatter.14.cloned.1.call-update) | async-done | bytes 393232 | tf_op jit(solution)/shard_map/reduce_scatter | solution.py:388
  561.6 40.4 %reduce-scatter.12.cloned.1.call-done = bf16[1,96,4096]{2,1,0:T(8,128)(2,1)} async-done(((bf16[1,768,4096]{2,1,0:T(8,128)(2,1)}), bf16[1,96,4096]{2,1,0:T(8,128)(2,1)}) %reduce-scatter.12.cloned.1.call-update) | async-done | bytes 786448 | tf_op jit(solution)/shard_map/reduce_scatter | solution.py:385
  (339 shorter events, 263.4 us)
Async XLA Ops:
  7.2 101.9 %all-gather.4.cloned.1.call-start = ((), (), s32[]{:S(2)}) async-start(), calls=%async_computation.11 | async-start | bytes 18229248 | tf_op jit(solution)/shard_map/all_gather | solution.py:131
  11.2 230.3 %all-gather.6.cloned.1.call-start = ((), (), s32[]{:S(2)}) async-start(), calls=%async_computation.12 | async-start | bytes 7077888 | tf_op jit(solution)/shard_map/all_gather | solution.py:160
  12.0 239.7 %all-gather.8.cloned.1.call-start = ((), (), s32[]{:S(2)}) async-start(), calls=%async_computation.13 | async-start | bytes 3538944 | tf_op jit(solution)/shard_map/all_gather | solution.py:161
  12.0 35.3 %collective-permute-start.7 = (s32[256]{0:T(256)}, s32[256]{0:T(256)S(1)}, u32[]{:S(2)}, u32[]{:S(2)}) collective-permute-start(s32[256]{0:T(256)} %bitcast.219), channel_id=1, source_target_pairs={{0,8},{8,16},{16,24},{24,32},{32,40},{40,48},{48,56},{56,64},{64,7... | collective-permute-start | bytes 3080 | tf_op jit(solution)/shard_map/ppermute | solution.py:18
  16.4 29.5 %collective-permute-start.6 = (s32[256]{0:T(256)}, s32[256]{0:T(256)S(1)}, u32[]{:S(2)}, u32[]{:S(2)}) collective-permute-start(s32[256]{0:T(256)} %bitcast.220), channel_id=1, source_target_pairs={{0,16},{8,24},{16,32},{24,40},{32,48},{40,56},{48,64},{56,72},{64,... | collective-permute-start | bytes 3080 | tf_op jit(solution)/shard_map/ppermute | solution.py:18
  21.6 22.4 %collective-permute-start.5 = (s32[256]{0:T(256)}, s32[256]{0:T(256)S(1)}, u32[]{:S(2)}, u32[]{:S(2)}) collective-permute-start(s32[256]{0:T(256)} %bitcast.221), channel_id=1, source_target_pairs={{0,24},{8,32},{16,40},{24,48},{32,56},{40,64},{48,72},{56,80},{64,... | collective-permute-start | bytes 3080 | tf_op jit(solution)/shard_map/ppermute | solution.py:18
  25.2 13.6 %collective-permute-start.4 = (s32[256]{0:T(256)}, s32[256]{0:T(256)S(1)}, u32[]{:S(2)}, u32[]{:S(2)}) collective-permute-start(s32[256]{0:T(256)} %bitcast.222), channel_id=1, source_target_pairs={{0,32},{8,40},{16,48},{24,56},{32,64},{40,72},{48,80},{56,88},{64,... | collective-permute-start | bytes 3080 | tf_op jit(solution)/shard_map/ppermute | solution.py:18
  28.3 24.0 %collective-permute-start.2 = (bf16[256,768]{1,0:T(8,128)(2,1)}, bf16[256,768]{1,0:T(8,128)(2,1)S(1)}, u32[]{:S(2)}, u32[]{:S(2)}) collective-permute-start(bf16[256,768]{1,0:T(8,128)(2,1)} %bitcast.194), channel_id=1, source_target_pairs={{0,16},{8,24},{16,32},{24,40},{32,48},{40,56},{48,64},{56,72},{64,... | collective-permute-start | bytes 1179656 | tf_op jit(solution)/shard_map/ppermute | solution.py:18
  202.3 32.1 %all-to-all-start = ((bf16[16,48,768]{2,1,0:T(8,128)(2,1)}), bf16[16,48,768]{2,1,0:T(8,128)(2,1)}, u32[]{:S(2)}, u32[]{:S(2)}) async-start(bf16[16,48,768]{2,1,0:T(8,128)(2,1)} %convolution_convert_fusion.7), calls=%async_computation | async-start | bytes 2359296 | tf_op jit(solution)/shard_map/all_to_all | solution.py:249
  208.6 256.4 %all-reduce.4.cloned.1.call-start = ((), (), s32[]{:S(2)}) async-start(), calls=%async_computation.18 | async-start | bytes 6291456
  234.4 23.8 %all-to-all-start.2 = ((bf16[16,48,768]{2,1,0:T(8,128)(2,1)}), bf16[16,48,768]{2,1,0:T(8,128)(2,1)}, u32[]{:S(2)}, u32[]{:S(2)}) async-start(bf16[16,48,768]{2,1,0:T(8,128)(2,1)} %bitcast.209), calls=%async_computation.2 | async-start | bytes 2359296 | tf_op jit(solution)/shard_map/all_to_all | solution.py:250
  273.0 19.8 %all-to-all-start.1 = ((bf16[16,48,768]{2,1,0:T(8,128)(2,1)}), bf16[16,48,768]{2,1,0:T(8,128)(2,1)}, u32[]{:S(2)}, u32[]{:S(2)}) async-start(bf16[16,48,768]{2,1,0:T(8,128)(2,1)} %bitcast.210), calls=%async_computation.1 | async-start | bytes 2359296 | tf_op jit(solution)/shard_map/all_to_all | solution.py:263
  292.8 20.7 %all-to-all-start.3 = ((bf16[16,48,768]{2,1,0:T(8,128)(2,1)}), bf16[16,48,768]{2,1,0:T(8,128)(2,1)}, u32[]{:S(2)}, u32[]{:S(2)}) async-start(bf16[16,48,768]{2,1,0:T(8,128)(2,1)} %bitcast.208), calls=%async_computation.3 | async-start | bytes 2359296 | tf_op jit(solution)/shard_map/all_to_all | solution.py:300
  298.2 187.7 %reduce-scatter.8.cloned.1.call-start = ((), (), s32[]{:S(2)}) async-start(), calls=%async_computation.14 | async-start | bytes 5529600 | tf_op jit(solution)/shard_map/reduce_scatter | solution.py:87
  376.2 14.7 %collective-permute-start.8 = (bf16[256,768]{1,0:T(8,128)(2,1)}, bf16[256,768]{1,0:T(8,128)(2,1)}, u32[]{:S(2)}, u32[]{:S(2)}) collective-permute-start(bf16[256,768]{1,0:T(8,128)(2,1)} %get-tuple-element.32), channel_id=1, source_target_pairs={{8,0},{16,8},{24,16},{32,24},{40,32},{48,40},{56,48},{64,56},{72,6... | collective-permute-start | bytes 1179656 | tf_op jit(solution)/shard_map/ppermute | solution.py:18
  377.5 15.3 %collective-permute-start.11 = (bf16[256,768]{1,0:T(8,128)(2,1)}, bf16[256,768]{1,0:T(8,128)(2,1)}, u32[]{:S(2)}, u32[]{:S(2)}) collective-permute-start(bf16[256,768]{1,0:T(8,128)(2,1)} %get-tuple-element.33), channel_id=1, source_target_pairs={{32,0},{40,8},{48,16},{56,24},{64,32},{72,40},{80,48},{88,56},{96,... | collective-permute-start | bytes 1179656 | tf_op jit(solution)/shard_map/ppermute | solution.py:18
  378.8 16.9 %collective-permute-start.10 = (bf16[256,768]{1,0:T(8,128)(2,1)}, bf16[256,768]{1,0:T(8,128)(2,1)}, u32[]{:S(2)}, u32[]{:S(2)}) collective-permute-start(bf16[256,768]{1,0:T(8,128)(2,1)} %get-tuple-element.34), channel_id=1, source_target_pairs={{24,0},{32,8},{40,16},{48,24},{56,32},{64,40},{72,48},{80,56},{88,... | collective-permute-start | bytes 1179656 | tf_op jit(solution)/shard_map/ppermute | solution.py:18
  380.1 15.7 %collective-permute-start.9 = (bf16[256,768]{1,0:T(8,128)(2,1)}, bf16[256,768]{1,0:T(8,128)(2,1)}, u32[]{:S(2)}, u32[]{:S(2)}) collective-permute-start(bf16[256,768]{1,0:T(8,128)(2,1)} %get-tuple-element.35), channel_id=1, source_target_pairs={{16,0},{24,8},{32,16},{40,24},{48,32},{56,40},{64,48},{72,56},{80,... | collective-permute-start | bytes 1179656 | tf_op jit(solution)/shard_map/ppermute | solution.py:18
  419.6 100.5 %reduce-scatter.10.cloned.1.call-start = ((), (), s32[]{:S(2)}) async-start(), calls=%async_computation.15 | async-start | bytes 7077888 | tf_op jit(solution)/shard_map/reduce_scatter | solution.py:87
  446.1 110.0 %reduce-scatter.14.cloned.1.call-start = ((), (), s32[]{:S(2)}) async-start(), calls=%async_computation.17 | async-start | bytes 3538944 | tf_op jit(solution)/shard_map/reduce_scatter | solution.py:388
  453.4 148.6 %reduce-scatter.12.cloned.1.call-start = ((), (), s32[]{:S(2)}) async-start(), calls=%async_computation.16 | async-start | bytes 7077888 | tf_op jit(solution)/shard_map/reduce_scatter | solution.py:385
  467.5 26.4 %all-to-all-start.6 = ((bf16[16,16,768]{2,1,0:T(8,128)(2,1)}), bf16[16,16,768]{2,1,0:T(8,128)(2,1)S(1)}, u32[]{:S(2)}, u32[]{:S(2)}) async-start(bf16[16,16,768]{2,1,0:T(8,128)(2,1)} %dynamic-slice_bitcast_fusion), calls=%async_computation.8 | async-start | bytes 786432 | tf_op jit(solution)/shard_map/all_to_all | solution.py:88
  493.9 28.8 %all-to-all-start.4 = ((bf16[16,6,3200]{2,1,0:T(8,128)(2,1)}), bf16[16,6,3200]{2,1,0:T(8,128)(2,1)S(1)}, u32[]{:S(2)}, u32[]{:S(2)}) async-start(bf16[16,6,3200]{2,1,0:T(8,128)(2,1)} %copy.97), calls=%async_computation.5 | async-start | bytes 1638400 | tf_op jit(solution)/shard_map/all_to_all | solution.py:88
  522.6 38.1 %all-to-all-start.5 = ((bf16[16,6,4096]{2,1,0:T(8,128)(2,1)}), bf16[16,6,4096]{2,1,0:T(8,128)(2,1)S(1)}, u32[]{:S(2)}, u32[]{:S(2)}) async-start(bf16[16,6,4096]{2,1,0:T(8,128)(2,1)} %copy.99), calls=%async_computation.7 | async-start | bytes 2097152 | tf_op jit(solution)/shard_map/all_to_all | solution.py:88
  (79 other events, 815.6 us)
Sparse Core Ops, SparseCore 0:
  11.6 97.4 all-gather.3
  110.8 40.3 all-gather.5
  152.9 27.8 all-gather.7
  224.9 68.5 all-reduce.3
  419.7 54.1 reduce-scatter.7
  476.2 43.8 reduce-scatter.9
  522.5 33.5 reduce-scatter.13
  558.5 43.4 reduce-scatter.11
